TPU v7x, 32 devices: a whole 2x2x4 slice. The times are simulated.
32 devices in a mesh: scene: 2 (over y), pts: 4 (over z), view: 2 (over x), head: 2 (over core).
Axes of the slice: x: 2, y: 2, z: 4, core: 2. Of those that a mesh axis runs over, the one named last changes fastest.
Arguments:
- queries: bfloat16 [2048, 1024], P(('scene', 'pts'), 'head'), parts along dimension 0, may hold values from -8 to 8
- key_tiles: bfloat16 [128, 16, 1024], P(('scene', 'pts', 'view'), None, 'head'), parts along dimension 0, may hold values from -4 to 4
- value_tiles: bfloat16 [128, 16, 1024], P(('scene', 'pts', 'view'), None, 'head'), parts along dimension 0, may hold values from -6 to 6
- visible: int32 [16, 32], P(('scene', 'pts'), 'view'), parts along dimension 0, may hold values from 0 to 63, as said below
- destination: int32 [2048], P(('scene', 'pts')), parts along dimension 0, may hold values from 0 to 1023, as said below
- d_out: bfloat16 [2048, 1024], P(('scene', 'pts'), 'head'), parts along dimension 0, may hold values from -6 to 6
Outputs:
- attended: bfloat16 [2048, 1024], P(('scene', 'pts'), 'head'), parts along dimension 0
- d_queries: bfloat16 [2048, 1024], P(('scene', 'pts'), 'head'), parts along dimension 0
- d_keys: bfloat16 [128, 16, 1024], P(('scene', 'pts', 'view'), None, 'head'), parts along dimension 0
- d_values: bfloat16 [128, 16, 1024], P(('scene', 'pts', 'view'), None, 'head'), parts along dimension 0
There are 2 independent parts, one for each index of `scene`. A program takes and returns all parts, laid end to end along the dimension named above; each array names one. Nothing has to cross between parts.
Inputs may be any that keep to these rules, and one draw needn't show every extreme that they name: `visible`: the 16 ids that one query block lists for view group v are distinct tiles held by devices of view index v. The lists of the query blocks of one pts index for one view group name exactly 32 distinct tiles, at most 8 of them held by any one device, and exactly 8 held by some device. `destination`: A permutation of the 1024 rows. The rows of each pts index go to the rows of every pts index, exactly 64 to each.
All inputs are finite; a program needn't handle non-finite values.
Results may differ from a plain program's by a relative error of at most 0.017.
Values may be sent and summed in bfloat16 or wider, within the bound.
A program may use at most 64 MiB of HBM per device.

v0:
```python
import math

import jax
import jax.numpy as jnp
from jax import lax
from jax.sharding import PartitionSpec as P

DH = 64
DIST = 32


HIGHEST = lax.Precision.HIGHEST


def merged(value, axis, join):
    pieces = jax.tree.map(lambda part: lax.all_gather(part, axis), value)
    head = jax.tree.map(lambda part: part[0], pieces)
    tail = jax.tree.map(lambda part: part[1:], pieces)
    running, _ = lax.scan(lambda running, share: (join(running, share), None), head, tail)
    return running


def fetch_tiles(requests, key_tiles, value_tiles):
    asked_ids = lax.all_to_all(requests, "pts", split_axis=0, concat_axis=0, tiled=True)
    safe_ids = jnp.maximum(asked_ids, 0)
    keys_out = jnp.take(key_tiles, safe_ids, axis=0)
    values_out = jnp.take(value_tiles, safe_ids, axis=0)
    keys_back = lax.all_to_all(keys_out, "pts", split_axis=0, concat_axis=0, tiled=True)
    values_back = lax.all_to_all(values_out, "pts", split_axis=0, concat_axis=0, tiled=True)
    return (keys_back, values_back, asked_ids)


def refetch_tiles(requests, key_tiles, value_tiles):
    safe_ids = jnp.maximum(
        lax.all_to_all(requests, "pts", split_axis=0, concat_axis=0, tiled=True), 0
    )
    keys_out = jnp.take(key_tiles, safe_ids, axis=0)
    values_out = jnp.take(value_tiles, safe_ids, axis=0)
    return (
        lax.all_to_all(keys_out, "pts", split_axis=0, concat_axis=0, tiled=True),
        lax.all_to_all(values_out, "pts", split_axis=0, concat_axis=0, tiled=True),
    )


def widen(stats):
    return jnp.repeat(stats, DH, axis=1)


def local(queries, key_tiles, value_tiles, visible, destination, d_out):
    pts_count = lax.axis_size("pts")
    view_count = lax.axis_size("view")
    kv_dev, tile_keys, local_width = key_tiles.shape
    qb_dev, nvis = visible.shape
    p_dev = queries.shape[0]
    qblock = p_dev // qb_dev
    heads_local = local_width // DH
    group_heads = math.gcd(heads_local, 4)
    group_width = group_heads * DH
    group_total = heads_local // group_heads
    capacity = max(2, min(kv_dev, 2 * DIST // pts_count))
    score_scale = DH ** (-0.5)
    slot_total = pts_count * capacity
    entries = visible.reshape(-1)
    entry_count = entries.shape[0]
    owner_of = entries // kv_dev // view_count
    local_id = entries % kv_dev
    positions = jnp.arange(entry_count)
    same_id = entries[:, None] == entries[None, :]
    earlier = positions[None, :] < positions[:, None]
    first_seen = jnp.logical_not(jnp.any(same_id & earlier, axis=1))
    same_owner = (owner_of[:, None] == owner_of[None, :]) & earlier & first_seen[None, :]
    owner_rank = jnp.sum(same_owner.astype(jnp.int32), axis=1)
    own_slot = owner_of * capacity + owner_rank
    slot_of = jnp.sum(jnp.where(same_id & first_seen[None, :], own_slot[None, :], 0), axis=1)
    slot_grid = jnp.arange(slot_total)
    slot_hit = (own_slot[None, :] == slot_grid[:, None]) & first_seen[None, :]
    requests = (jnp.sum(jnp.where(slot_hit, local_id[None, :] + 1, 0), axis=1) - 1).reshape(
        pts_count, capacity
    )
    slot_table = slot_of.reshape(qb_dev, nvis)

    def block_tiles(fetched):
        flat_tiles = fetched.reshape(slot_total, tile_keys, local_width)
        return jnp.take(flat_tiles, slot_table, axis=0).reshape(
            qb_dev, nvis * tile_keys, local_width
        )

    fetched_keys, fetched_values, asked = fetch_tiles(requests, key_tiles, value_tiles)
    block_keys = block_tiles(fetched_keys)
    block_values = block_tiles(fetched_values)
    query_blocks = queries.reshape(qb_dev, qblock, local_width)
    key_count = nvis * tile_keys
    peak_list, total_list, weighted_list = ([], [], [])
    for group_number in range(group_total):
        col_start = group_number * group_width
        col_stop = col_start + group_width
        query_part = query_blocks[..., col_start:col_stop].reshape(qb_dev, qblock, group_heads, DH)
        key_part = block_keys[..., col_start:col_stop].reshape(qb_dev, key_count, group_heads, DH)
        value_part = block_values[..., col_start:col_stop].reshape(
            qb_dev, key_count, group_heads, DH
        )
        scores = (
            jnp.einsum("bqhd,bkhd->bhqk", query_part, key_part, preferred_element_type=jnp.float32)
            * score_scale
        )
        local_peak = jnp.max(scores, axis=-1)
        exponent = jnp.exp(scores - local_peak[..., None])
        local_total = jnp.sum(exponent, axis=-1)
        weighted = jnp.einsum(
            "bhqk,bkhd->bqhd",
            exponent.astype(jnp.bfloat16),
            value_part,
            preferred_element_type=jnp.float32,
        )
        peak_list.append(jnp.transpose(local_peak, (0, 2, 1)))
        total_list.append(jnp.transpose(local_total, (0, 2, 1)))
        weighted_list.append(weighted.reshape(qb_dev, qblock, group_width))
    peak_rows = jnp.concatenate(peak_list, axis=-1).reshape(p_dev, heads_local)
    total_rows = jnp.concatenate(total_list, axis=-1).reshape(p_dev, heads_local)
    weighted_rows = jnp.concatenate(weighted_list, axis=-1).reshape(p_dev, local_width)

    def join(first_part, second_part):
        peak_a, total_a, sum_a = first_part
        peak_b, total_b, sum_b = second_part
        peak_top = jnp.maximum(peak_a, peak_b)
        factor_a = jnp.exp(peak_a - peak_top)
        factor_b = jnp.exp(peak_b - peak_top)
        return (
            peak_top,
            factor_a * total_a + factor_b * total_b,
            widen(factor_a) * sum_a + widen(factor_b) * sum_b,
        )

    big_peak, big_total, big_sum = merged((peak_rows, total_rows, weighted_rows), "view", join)
    attended_rows = (big_sum / widen(big_total)).astype(jnp.bfloat16)
    again_keys, again_values = refetch_tiles(requests, key_tiles, value_tiles)
    grad_keys = block_tiles(again_keys)
    grad_values = block_tiles(again_values)
    delta_rows = jnp.sum(
        (d_out.astype(jnp.float32) * attended_rows.astype(jnp.float32)).reshape(
            p_dev, heads_local, DH
        ),
        axis=-1,
    )
    peak_heads = big_peak.reshape(qb_dev, qblock, heads_local)
    total_heads = big_total.reshape(qb_dev, qblock, heads_local)
    delta_heads = delta_rows.reshape(qb_dev, qblock, heads_local)
    grad_blocks = d_out.reshape(qb_dev, qblock, local_width)
    dquery_list, dkey_list, dvalue_list = ([], [], [])
    for group_number in range(group_total):
        col_start = group_number * group_width
        col_stop = col_start + group_width
        head_start = group_number * group_heads
        head_stop = head_start + group_heads
        query_part = query_blocks[..., col_start:col_stop].reshape(qb_dev, qblock, group_heads, DH)
        key_part = grad_keys[..., col_start:col_stop].reshape(qb_dev, key_count, group_heads, DH)
        value_part = grad_values[..., col_start:col_stop].reshape(
            qb_dev, key_count, group_heads, DH
        )
        grad_part = grad_blocks[..., col_start:col_stop].reshape(qb_dev, qblock, group_heads, DH)
        peak_part = jnp.transpose(peak_heads[..., head_start:head_stop], (0, 2, 1))[..., None]
        total_part = jnp.transpose(total_heads[..., head_start:head_stop], (0, 2, 1))[..., None]
        delta_part = jnp.transpose(delta_heads[..., head_start:head_stop], (0, 2, 1))[..., None]
        scores = (
            jnp.einsum("bqhd,bkhd->bhqk", query_part, key_part, preferred_element_type=jnp.float32)
            * score_scale
        )
        probability = jnp.exp(scores - peak_part) / total_part
        value_grad = jnp.einsum(
            "bhqk,bqhd->bkhd",
            probability.astype(jnp.bfloat16),
            grad_part,
            preferred_element_type=jnp.float32,
        )
        d_prob = jnp.einsum(
            "bqhd,bkhd->bhqk", grad_part, value_part, preferred_element_type=jnp.float32
        )
        d_score = (probability * (d_prob - delta_part)).astype(jnp.bfloat16)
        query_grad = (
            jnp.einsum("bhqk,bkhd->bqhd", d_score, key_part, preferred_element_type=jnp.float32)
            * score_scale
        )
        key_grad = (
            jnp.einsum("bhqk,bqhd->bkhd", d_score, query_part, preferred_element_type=jnp.float32)
            * score_scale
        )
        dquery_list.append(query_grad.reshape(qb_dev, qblock, group_width))
        dkey_list.append(key_grad.reshape(qb_dev, key_count, group_width))
        dvalue_list.append(value_grad.reshape(qb_dev, key_count, group_width))
    dquery_local = jnp.concatenate(dquery_list, axis=-1).reshape(p_dev, local_width)
    dkey_blocks = jnp.concatenate(dkey_list, axis=-1)
    dvalue_blocks = jnp.concatenate(dvalue_list, axis=-1)
    d_queries = lax.psum(dquery_local, "view").astype(jnp.bfloat16)
    slot_match = (slot_of[None, :] == slot_grid[:, None]).astype(jnp.float32)

    def per_slot(blocks):
        flat_rows = blocks.reshape(qb_dev * nvis, tile_keys * local_width)
        summed = jnp.dot(
            slot_match, flat_rows, precision=HIGHEST, preferred_element_type=jnp.float32
        )
        return summed.astype(jnp.bfloat16).reshape(pts_count, capacity, tile_keys, local_width)

    back_keys, back_values = (
        lax.all_to_all(per_slot(dkey_blocks), "pts", split_axis=0, concat_axis=0, tiled=True),
        lax.all_to_all(per_slot(dvalue_blocks), "pts", split_axis=0, concat_axis=0, tiled=True),
    )
    owner_match = (asked.reshape(-1)[None, :] == jnp.arange(kv_dev)[:, None]).astype(jnp.bfloat16)
    d_keys = (
        jnp.dot(
            owner_match,
            back_keys.reshape(slot_total, tile_keys * local_width),
            preferred_element_type=jnp.float32,
        )
        .astype(jnp.bfloat16)
        .reshape(kv_dev, tile_keys, local_width)
    )
    d_values = (
        jnp.dot(
            owner_match,
            back_values.reshape(slot_total, tile_keys * local_width),
            preferred_element_type=jnp.float32,
        )
        .astype(jnp.bfloat16)
        .reshape(kv_dev, tile_keys, local_width)
    )
    per_peer = p_dev // pts_count
    target = destination // p_dev
    row_place = destination % p_dev
    peer_hits = (target[:, None] == jnp.arange(pts_count)[None, :]).astype(jnp.int32)
    before = jnp.cumsum(peer_hits, axis=0) - peer_hits
    send_rank = jnp.sum(before * peer_hits, axis=1)
    send_position = target * per_peer + send_rank
    row_numbers = jnp.arange(p_dev, dtype=jnp.int32)
    send_inverse = jnp.zeros((p_dev,), jnp.int32).at[send_position].set(row_numbers)
    rows_out = attended_rows[send_inverse].reshape(pts_count, per_peer, local_width)
    places_out = row_place[send_inverse].reshape(pts_count, per_peer)
    got_rows, got_places = (
        lax.all_to_all(rows_out, "pts", split_axis=0, concat_axis=0, tiled=True),
        lax.all_to_all(places_out, "pts", split_axis=0, concat_axis=0, tiled=True),
    )
    place_inverse = jnp.zeros((p_dev,), jnp.int32).at[got_places.reshape(-1)].set(row_numbers)
    attended = got_rows.reshape(p_dev, local_width)[place_inverse]
    return (attended, d_queries, d_keys, d_values)


def solution(mesh):
    in_specs = (
        P(("scene", "pts"), "head"),
        P(("scene", "pts", "view"), None, "head"),
        P(("scene", "pts", "view"), None, "head"),
        P(("scene", "pts"), "view"),
        P(("scene", "pts")),
        P(("scene", "pts"), "head"),
    )
    out_specs = (
        P(("scene", "pts"), "head"),
        P(("scene", "pts"), "head"),
        P(("scene", "pts", "view"), None, "head"),
        P(("scene", "pts", "view"), None, "head"),
    )
    return jax.shard_map(local, mesh=mesh, in_specs=in_specs, out_specs=out_specs, check_vma=False)
```

profile of v0, /device:TPU:0, one launch (start us, length us, event | category | flops | bytes accessed | tf_op | source)
XLA Modules:
  0.0 160.3 jit_solution(14383902787130595014)
XLA Ops:
  9.2 6.4 %all-to-all-start = ((s32[4,1,8]{2,1,0:T(1,128)}), s32[4,1,8]{2,1,0:T(1,128)S(1)}, u32[]{:S(2)}, u32[]{:S(2)}) async-start(s32[4,1,8]{2,1,0:T(1,128)} %bitcast), calls=%async_computation | async-start | bytes 4096 | tf_op jit(solution)/shard_map/all_to_all | solution.py:24
  17.4 3.7 %all-to-all-done = s32[4,1,8]{2,1,0:T(1,128)S(1)} async-done(((s32[4,1,8]{2,1,0:T(1,128)}), s32[4,1,8]{2,1,0:T(1,128)S(1)}, u32[]{:S(2)}, u32[]{:S(2)}) %all-to-all-start) | async-done | bytes 160 | tf_op jit(solution)/shard_map/all_to_all | solution.py:24
  25.7 3.6 %all-to-all-start.2 = ((bf16[4,8,16,512]{3,2,1,0:T(8,128)(2,1)}), bf16[4,8,16,512]{3,2,1,0:T(8,128)(2,1)S(1)}, u32[]{:S(2)}, u32[]{:S(2)}) async-start(bf16[4,8,16,512]{3,2,1,0:T(8,128)(2,1)} %get-tuple-element.72), calls=%async_computation.2 | async-start | bytes 1048576 | tf_op jit(solution)/shard_map/all_to_all | solution.py:29
  29.4 1.4 scatter_custom_fusion
  30.8 11.8 %all-to-all-done.2 = bf16[4,8,16,512]{3,2,1,0:T(8,128)(2,1)S(1)} async-done(((bf16[4,8,16,512]{3,2,1,0:T(8,128)(2,1)}), bf16[4,8,16,512]{3,2,1,0:T(8,128)(2,1)S(1)}, u32[]{:S(2)}, u32[]{:S(2)}) %all-to-all-start.2) | async-done | bytes 524320 | tf_op jit(solution)/shard_map/all_to_all | solution.py:29
  42.6 3.5 %all-to-all-start.1 = ((bf16[4,8,16,512]{3,2,1,0:T(8,128)(2,1)}), bf16[4,8,16,512]{3,2,1,0:T(8,128)(2,1)S(1)}, u32[]{:S(2)}, u32[]{:S(2)}) async-start(bf16[4,8,16,512]{3,2,1,0:T(8,128)(2,1)} %get-tuple-element.73), calls=%async_computation.1 | async-start | bytes 1048576 | tf_op jit(solution)/shard_map/all_to_all | solution.py:28
  46.5 1.9 %gather_fusion.1 = s32[256]{0:T(256)S(1)} fusion(s32[256]{0:T(256)S(1)} %get-tuple-element.68, s32[1024]{0:T(1024)S(1)} %pad_clamp_fusion.1), kind=kCustom, calls=%fused_computation.5 | custom fusion | bytes 3072 | tf_op jit(solution)/shard_map/gather | solution.py:236
  51.3 8.6 %all-to-all-done.1 = bf16[4,8,16,512]{3,2,1,0:T(8,128)(2,1)S(1)} async-done(((bf16[4,8,16,512]{3,2,1,0:T(8,128)(2,1)}), bf16[4,8,16,512]{3,2,1,0:T(8,128)(2,1)S(1)}, u32[]{:S(2)}, u32[]{:S(2)}) %all-to-all-start.1) | async-done | bytes 524320 | tf_op jit(solution)/shard_map/all_to_all | solution.py:28
  59.9 3.8 %all-to-all-start.4 = ((s32[4,1,64]{2,1,0:T(1,128)}), s32[4,1,64]{2,1,0:T(1,128)}, u32[]{:S(2)}, u32[]{:S(2)}) async-start(s32[4,1,64]{2,1,0:T(1,128)} %all_to_all.32), calls=%async_computation.4 | async-start | bytes 4096 | tf_op jit(solution)/shard_map/all_to_all | solution.py:239
  66.5 4.4 %all_gather.11 = f32[2,256,8]{1,2,0:T(8,128)S(1)} all-gather(f32[1,256,8]{1,2,0:T(8,128)S(1)} %maximum_bitcast_fusion.1), channel_id=1, replica_groups=mesh['scene'=2,'pts'=4,'view'=2,'head'=2] {'view'}, dimensions={0}, use_global_device_ids=true | all-gather | bytes 24576 | tf_op jit(solution)/shard_map/all_gather | solution.py:16
  70.9 4.5 %all_gather.9 = f32[2,256,8]{1,2,0:T(8,128)} all-gather(f32[1,256,8]{1,2,0:T(8,128)S(1)} %maximum_bitcast_fusion), channel_id=1, replica_groups=mesh['scene'=2,'pts'=4,'view'=2,'head'=2] {'view'}, dimensions={0}, use_global_device_ids=true | all-gather | bytes 24576 | tf_op jit(solution)/shard_map/all_gather | solution.py:16
  87.1 2.7 %convolution_convert_fusion = bf16[32,8192]{1,0:T(8,128)(2,1)} fusion(f32[32,8192]{1,0:T(8,128)} %reshape.397, s32[32]{0:T(128)} %copy-done.27), kind=kOutput, calls=%fused_computation.9 | convolution fusion | flops 100926464 | bytes 1572992 | tf_op jit(solution)/shard_map/dot_general | solution.py:198
  89.8 5.1 %all-to-all-start.6 = ((bf16[4,8,16,512]{3,1,2,0:T(8,128)(2,1)}), bf16[4,8,16,512]{3,1,2,0:T(8,128)(2,1)S(1)}, u32[]{:S(2)}, u32[]{:S(2)}) async-start(bf16[4,8,16,512]{3,1,2,0:T(8,128)(2,1)} %bitcast.72), calls=%async_computation.6 | async-start | bytes 1048576 | tf_op jit(solution)/shard_map/all_to_all | solution.py:205
  97.0 1.6 scatter_custom_fusion.1
  102.7 2.0 %copy.109 = f32[256,512]{1,0:T(8,128)} copy(f32[256,512]{0,1:T(8,128)} %bitcast.232) | data formatting | bytes 1048576 | tf_op jit(solution)/shard_map/while/body/eval_jaxpr/reshape | solution.py:46
  105.6 2.0 %copy.108 = f32[256,512]{1,0:T(8,128)} copy(f32[256,512]{0,1:T(8,128)} %bitcast.233) | data formatting | bytes 1048576 | tf_op jit(solution)/shard_map/while/body/eval_jaxpr/reshape | solution.py:46
  109.5 2.6 %convert_multiply_fusion = (f32[256,512]{1,0:T(8,128)}, bf16[256,512]{1,0:T(8,128)(2,1)S(1)}) fusion(bf16[256,512]{1,0:T(8,128)(2,1)S(1)} %copy-done.9, f32[256,512]{1,0:T(8,128)S(1)} %copy.110, f32[256,512]{1,0:T(8,128)} %copy.109, f32[2,256,512]{2,1,0:T(8,128)} %all-gather.2.cloned.1.call-done, f32[256,512]{1,0:T(8,128)} %copy.108), kind=kLoop, calls=%fused_computation.56 | loop fusion | flops 1048576 | bytes 3670016 | tf_op jit(solution)/shard_map/mul | solution.py:140
  116.5 2.0 %gather_fusion = bf16[256,512]{1,0:T(8,128)(2,1)} fusion(bf16[256,512]{1,0:T(8,128)(2,1)S(1)} %get-tuple-element.48, s32[1024]{0:T(1024)} %copy-done.25), kind=kCustom, calls=%fused_computation.4 | custom fusion | bytes 525312 | tf_op jit(solution)/shard_map/gather | solution.py:235
  118.5 5.1 %all-to-all-start.3 = ((bf16[4,64,512]{2,1,0:T(8,128)(2,1)}), bf16[4,64,512]{2,1,0:T(8,128)(2,1)S(1)}, u32[]{:S(2)}, u32[]{:S(2)}) async-start(bf16[4,64,512]{2,1,0:T(8,128)(2,1)} %bitcast.39), calls=%async_computation.3 | async-start | bytes 524288 | tf_op jit(solution)/shard_map/all_to_all | solution.py:238
  127.5 1.4 convolution_convert_fusion.1
  128.9 1.5 all-to-all-done.3
  130.4 3.6 %all-to-all-start.5 = ((bf16[4,8,16,512]{3,1,2,0:T(8,128)(2,1)}), bf16[4,8,16,512]{3,1,2,0:T(8,128)(2,1)S(1)}, u32[]{:S(2)}, u32[]{:S(2)}) async-start(bf16[4,8,16,512]{3,1,2,0:T(8,128)(2,1)} %bitcast.65), calls=%async_computation.5 | async-start | bytes 1048576 | tf_op jit(solution)/shard_map/all_to_all | solution.py:204
  134.5 15.3 %all-reduce.1 = bf16[256,512]{0,1:T(8,128)(2,1)S(1)} all-reduce(f32[256,512]{0,1:T(8,128)S(1)} %pad_maximum_fusion.3), channel_id=1, replica_groups=mesh['scene'=2,'pts'=4,'view'=2,'head'=2] {'view'}, use_global_device_ids=true, to_apply=%region_14.17 | all-reduce | flops 131072 | bytes 786432 | tf_op jit(solution)/shard_map/psum | solution.py:193
  150.6 2.0 %gather_fusion.2 = bf16[256,512]{1,0:T(8,128)(2,1)} fusion(bf16[256,512]{1,0:T(8,128)(2,1)S(1)} %bitcast.215, s32[1024]{0:T(1024)} %pad_clamp_fusion), kind=kCustom, calls=%fused_computation.6 | custom fusion | bytes 525312 | tf_op jit(solution)/shard_map/gather | solution.py:242
  (194 shorter events, 45.0 us)
Async XLA Ops:
  7.2 15.9 %copy-start = (bf16[8,16,512]{2,1,0:T(8,128)(2,1)S(1)}, bf16[8,16,512]{2,1,0:T(8,128)(2,1)}, u32[]{:S(2)}) copy-start(bf16[8,16,512]{2,1,0:T(8,128)(2,1)} %param.12) | copy-start | bytes 393220
  8.6 8.8 %copy-start.27 = (s32[32]{0:T(128)}, s32[32]{0:T(128)S(1)}, u32[]{:S(2)}) copy-start(s32[32]{0:T(128)S(1)} %get-tuple-element.43) | copy-start | bytes 388
  9.2 6.5 %copy-start.38 = (s32[256]{0:T(256)S(1)}, s32[256]{0:T(256)}, u32[]{:S(2)}) copy-start(s32[256]{0:T(256)} %param.14) | copy-start | bytes 3076
  9.2 11.9 %all-to-all-start = ((s32[4,1,8]{2,1,0:T(1,128)}), s32[4,1,8]{2,1,0:T(1,128)S(1)}, u32[]{:S(2)}, u32[]{:S(2)}) async-start(s32[4,1,8]{2,1,0:T(1,128)} %bitcast), calls=%async_computation | async-start | bytes 4096 | tf_op jit(solution)/shard_map/all_to_all | solution.py:24
  25.7 5.1 %copy-start.14 = (bf16[256,512]{1,0:T(8,128)(2,1)S(1)}, bf16[256,512]{1,0:T(8,128)(2,1)}, u32[]{:S(2)}) copy-start(bf16[256,512]{1,0:T(8,128)(2,1)} %param.10) | copy-start | bytes 786436
  25.7 16.9 %all-to-all-start.2 = ((bf16[4,8,16,512]{3,2,1,0:T(8,128)(2,1)}), bf16[4,8,16,512]{3,2,1,0:T(8,128)(2,1)S(1)}, u32[]{:S(2)}, u32[]{:S(2)}) async-start(bf16[4,8,16,512]{3,2,1,0:T(8,128)(2,1)} %get-tuple-element.72), calls=%async_computation.2 | async-start | bytes 1048576 | tf_op jit(solution)/shard_map/all_to_all | solution.py:29
  42.6 17.3 %all-to-all-start.1 = ((bf16[4,8,16,512]{3,2,1,0:T(8,128)(2,1)}), bf16[4,8,16,512]{3,2,1,0:T(8,128)(2,1)S(1)}, u32[]{:S(2)}, u32[]{:S(2)}) async-start(bf16[4,8,16,512]{3,2,1,0:T(8,128)(2,1)} %get-tuple-element.73), calls=%async_computation.1 | async-start | bytes 1048576 | tf_op jit(solution)/shard_map/all_to_all | solution.py:28
  46.3 18.5 %copy-start.6 = (bf16[2,128,256]{1,2,0:T(8,128)(2,1)}, bf16[2,128,256]{1,2,0:T(8,128)(2,1)S(1)}, u32[]{:S(2)}) copy-start(bf16[2,128,256]{1,2,0:T(8,128)(2,1)S(1)} %copy.140) | copy-start | bytes 393220
  46.5 19.4 %copy-start.4 = (bf16[2,128,256]{1,2,0:T(8,128)(2,1)}, bf16[2,128,256]{1,2,0:T(8,128)(2,1)S(1)}, u32[]{:S(2)}) copy-start(bf16[2,128,256]{1,2,0:T(8,128)(2,1)S(1)} %copy.139) | copy-start | bytes 393220
  46.5 2.0 %copy-start.25 = (s32[1024]{0:T(1024)}, s32[1024]{0:T(1024)S(1)}, u32[]{:S(2)}) copy-start(s32[1024]{0:T(1024)S(1)} %pad_clamp_fusion.1) | copy-start | bytes 12292
  46.5 2.6 %copy-start.8 = (bf16[256,512]{1,0:T(8,128)(2,1)S(1)}, bf16[256,512]{1,0:T(8,128)(2,1)}, u32[]{:S(2)}) copy-start(bf16[256,512]{1,0:T(8,128)(2,1)} %param.15) | copy-start | bytes 786436
  59.9 29.9 %all-to-all-start.4 = ((s32[4,1,64]{2,1,0:T(1,128)}), s32[4,1,64]{2,1,0:T(1,128)}, u32[]{:S(2)}, u32[]{:S(2)}) async-start(s32[4,1,64]{2,1,0:T(1,128)} %all_to_all.32), calls=%async_computation.4 | async-start | bytes 4096 | tf_op jit(solution)/shard_map/all_to_all | solution.py:239
  63.7 45.6 %all-gather.2.cloned.1.call-start = ((), (), s32[]{:S(2)}) async-start(), calls=%async_computation.7 | async-start | bytes 1572864 | tf_op jit(solution)/shard_map/all_gather | solution.py:16
  65.7 5.1 %copy-start.22 = (f32[2,4,128]{2,1,0:T(4,128)}, f32[2,4,128]{2,1,0:T(4,128)S(1)}, u32[]{:S(2)}) copy-start(f32[2,4,128]{2,1,0:T(4,128)S(1)} %get-tuple-element.76) | copy-start | bytes 12292
  66.3 4.6 %copy-start.21 = (f32[2,4,128]{2,1,0:T(4,128)}, f32[2,4,128]{2,1,0:T(4,128)S(1)}, u32[]{:S(2)}) copy-start(f32[2,4,128]{2,1,0:T(4,128)S(1)} %get-tuple-element.78) | copy-start | bytes 12292
  81.7 1.6 copy-start.30
  81.7 1.6 copy-start.32
  89.8 5.1 %copy-start.26 = (s32[4,8]{1,0:T(4,128)S(1)}, s32[4,8]{1,0:T(4,128)}, u32[]{:S(2)}) copy-start(s32[4,8]{1,0:T(4,128)} %get-tuple-element.66) | copy-start | bytes 388
  89.8 17.9 %all-to-all-start.6 = ((bf16[4,8,16,512]{3,1,2,0:T(8,128)(2,1)}), bf16[4,8,16,512]{3,1,2,0:T(8,128)(2,1)S(1)}, u32[]{:S(2)}, u32[]{:S(2)}) async-start(bf16[4,8,16,512]{3,1,2,0:T(8,128)(2,1)} %bitcast.72), calls=%async_computation.6 | async-start | bytes 1048576 | tf_op jit(solution)/shard_map/all_to_all | solution.py:205
  94.9 4.3 %copy-start.16 = (f32[2,256,8]{1,2,0:T(8,128)S(1)}, f32[2,256,8]{1,2,0:T(8,128)}, u32[]{:S(2)}) copy-start(f32[2,256,8]{1,2,0:T(8,128)} %all_gather.9) | copy-start | bytes 49156
  100.6 1.3 copy-start.24
  102.7 2.0 %copy-start.23 = (f32[256,8]{0,1:T(8,128)S(1)}, f32[256,8]{0,1:T(8,128)}, u32[]{:S(2)}) copy-start(f32[256,8]{0,1:T(8,128)} %get-tuple-element.50) | copy-start | bytes 24580
  118.5 11.9 %all-to-all-start.3 = ((bf16[4,64,512]{2,1,0:T(8,128)(2,1)}), bf16[4,64,512]{2,1,0:T(8,128)(2,1)S(1)}, u32[]{:S(2)}, u32[]{:S(2)}) async-start(bf16[4,64,512]{2,1,0:T(8,128)(2,1)} %bitcast.39), calls=%async_computation.3 | async-start | bytes 524288 | tf_op jit(solution)/shard_map/all_to_all | solution.py:238
  130.4 22.2 %all-to-all-start.5 = ((bf16[4,8,16,512]{3,1,2,0:T(8,128)(2,1)}), bf16[4,8,16,512]{3,1,2,0:T(8,128)(2,1)S(1)}, u32[]{:S(2)}, u32[]{:S(2)}) async-start(bf16[4,8,16,512]{3,1,2,0:T(8,128)(2,1)} %bitcast.65), calls=%async_computation.5 | async-start | bytes 1048576 | tf_op jit(solution)/shard_map/all_to_all | solution.py:204
  (23 other events, 19.5 us)
Sparse Core Ops, SparseCore 0:
  81.1 22.6 all-gather.1
where the time goes:
time: 161 us; the launch traced here: 160 us
  local copies, waits for them, and re-layouts  43.3 us (27%)
  starting transfers between devices  31.1 us (19%)
  waiting for transfers between devices  25.7 us (16%)
  blocking collectives  24.1 us (15%)
  between operations  14.8 us (9%)
  other arithmetic  11.7 us (7%)
  matrix products  9.66 us (6%)
    psum x1, blocking collectives, local(): d_queries = lax.psum(dquery_local, 'view').astype(jnp.bfloat16)  15.3 us
    unnamed x87, local copies, waits for them, and re-layouts  12.4 us
    all_to_all x1, waiting for transfers between devices, fetch_tiles(): lax.all_to_all(values_out, 'pts', split_axis=0, concat_axis=0, tiled=True)  11.8 us
    all_gather x2, blocking collectives, merged(): pieces = jax.tree.map(lambda part: lax.all_gather(part, axis), value)  8.84 us
    all_to_all x1, waiting for transfers between devices, fetch_tiles(): lax.all_to_all(keys_out, 'pts', split_axis=0, concat_axis=0, tiled=True)  8.62 us
    all_to_all x1, starting transfers between devices, fetch_tiles(): lax.all_to_all(requests, 'pts', split_axis=0, concat_axis=0, tiled=True)  6.45 us
    reshape x3, local copies, waits for them, and re-layouts, widen(): return jnp.repeat(stats, DH, axis=1)  5.34 us
    all_to_all x1, starting transfers between devices, local(): lax.all_to_all(per_slot(dvalue_blocks), 'pts', split_axis=0, concat_axis=...  5.14 us
  transfers between devices with their start and end apart: 8, of which 4 were waited for; matrix products, arithmetic and copies ran while one was open for 26% of the time, Pallas kernels for 0%

commit v1 on v0

--- a/solution.py
+++ b/solution.py
@@ -1,11 +1,15 @@
+import functools
 import math
 
 import jax
 import jax.numpy as jnp
 from jax import lax
+from jax.experimental import pallas as pl
+from jax.experimental.pallas import tpu as pltpu
 from jax.sharding import PartitionSpec as P
 
 DH = 64
+HEADS = 16
 DIST = 32
 
 
@@ -20,11 +24,19 @@
     return running
 
 
+def pick(table, ids):
+    hits = (ids.reshape(-1)[:, None] == jnp.arange(table.shape[0])[None, :]).astype(jnp.bfloat16)
+    flat = jnp.dot(
+        hits, table.reshape(table.shape[0], -1), preferred_element_type=jnp.float32
+    ).astype(table.dtype)
+    return flat.reshape(ids.shape + table.shape[1:])
+
+
 def fetch_tiles(requests, key_tiles, value_tiles):
     asked_ids = lax.all_to_all(requests, "pts", split_axis=0, concat_axis=0, tiled=True)
     safe_ids = jnp.maximum(asked_ids, 0)
-    keys_out = jnp.take(key_tiles, safe_ids, axis=0)
-    values_out = jnp.take(value_tiles, safe_ids, axis=0)
+    keys_out = pick(key_tiles, safe_ids)
+    values_out = pick(value_tiles, safe_ids)
     keys_back = lax.all_to_all(keys_out, "pts", split_axis=0, concat_axis=0, tiled=True)
     values_back = lax.all_to_all(values_out, "pts", split_axis=0, concat_axis=0, tiled=True)
     return (keys_back, values_back, asked_ids)
@@ -34,8 +46,8 @@
     safe_ids = jnp.maximum(
         lax.all_to_all(requests, "pts", split_axis=0, concat_axis=0, tiled=True), 0
     )
-    keys_out = jnp.take(key_tiles, safe_ids, axis=0)
-    values_out = jnp.take(value_tiles, safe_ids, axis=0)
+    keys_out = pick(key_tiles, safe_ids)
+    values_out = pick(value_tiles, safe_ids)
     return (
         lax.all_to_all(keys_out, "pts", split_axis=0, concat_axis=0, tiled=True),
         lax.all_to_all(values_out, "pts", split_axis=0, concat_axis=0, tiled=True),
@@ -81,7 +93,7 @@
 
     def block_tiles(fetched):
         flat_tiles = fetched.reshape(slot_total, tile_keys, local_width)
-        return jnp.take(flat_tiles, slot_table, axis=0).reshape(
+        return pick(flat_tiles, slot_table).reshape(
             qb_dev, nvis * tile_keys, local_width
         )
 
@@ -227,7 +239,12 @@
     target = destination // p_dev
     row_place = destination % p_dev
     peer_hits = (target[:, None] == jnp.arange(pts_count)[None, :]).astype(jnp.int32)
-    before = jnp.cumsum(peer_hits, axis=0) - peer_hits
+    ahead = jnp.arange(p_dev)[None, :] < jnp.arange(p_dev)[:, None]
+    before = jnp.dot(
+        ahead.astype(jnp.bfloat16),
+        peer_hits.astype(jnp.bfloat16),
+        preferred_element_type=jnp.float32,
+    ).astype(jnp.int32)
     send_rank = jnp.sum(before * peer_hits, axis=1)
     send_position = target * per_peer + send_rank
     row_numbers = jnp.arange(p_dev, dtype=jnp.int32)
@@ -243,6 +260,289 @@
     return (attended, d_queries, d_keys, d_values)
 
 
+MESH = pl.DeviceIdType.MESH
+WIDE = 2 * DH
+TILE = 16
+HIDDEN = -1e30
+META_ROWS = 8
+
+
+def remote(src, dst, send_sem, recv_sem, place):
+    return pltpu.make_async_remote_copy(
+        src_ref=src,
+        dst_ref=dst,
+        send_sem=send_sem,
+        recv_sem=recv_sem,
+        device_id=place,
+        device_id_type=MESH,
+    )
+
+
+def head_kernel(
+    pts,
+    view,
+    q_ref,
+    k_ref,
+    v_ref,
+    vis_ref,
+    dest_ref,
+    g_ref,
+    att_ref,
+    dq_ref,
+    dk_ref,
+    dv_ref,
+    meta,
+    kv_out,
+    kv,
+    qd_out,
+    qd,
+    bias,
+    place,
+    rows,
+    grads,
+    od_out,
+    od,
+    dkv_out,
+    dkv,
+    meta_s,
+    meta_r,
+    kv_s,
+    kv_r,
+    qd_s,
+    qd_r,
+    od_s,
+    od_r,
+    dkv_s,
+    dkv_r,
+):
+    z = lax.axis_index("pts")
+    w = lax.axis_index("view")
+    peers = pts * view
+    me = z * view + w
+    p_dev = q_ref.shape[0]
+    qb_dev, nvis = vis_ref.shape
+    qblock = p_dev // qb_dev
+    held = k_ref.shape[0]
+    keys = peers * held
+    dest_rows = dest_ref.shape[0]
+
+    barrier = pltpu.get_barrier_semaphore()
+    others = []
+    for step in range(1, peers):
+        other = lax.rem(me + step, peers)
+        others.append((other, other // view, lax.rem(other, view)))
+    column = []
+    for step in range(1, pts):
+        column.append(lax.rem(z + step, pts))
+    for _, oz, ow in others:
+        pl.semaphore_signal(barrier, inc=1, device_id={"pts": oz, "view": ow}, device_id_type=MESH)
+
+    meta[me] = jnp.zeros((META_ROWS, WIDE), jnp.int32)
+    meta[me, 0:qb_dev, 0:nvis] = vis_ref[...]
+    meta[me, qb_dev : qb_dev + dest_rows, :] = dest_ref[...]
+    for pair in range(peers // 2):
+        cols = slice(pair * WIDE, (pair + 1) * WIDE)
+        kt, vt = k_ref[:, cols], v_ref[:, cols]
+        kv_out[2 * pair] = jnp.concatenate([kt[:, :DH], vt[:, :DH]], axis=1)
+        kv_out[2 * pair + 1] = jnp.concatenate([kt[:, DH:], vt[:, DH:]], axis=1)
+    pl.semaphore_wait(barrier, peers - 1)
+
+    sends = []
+
+    def start(copy):
+        copy.start()
+        sends.append(copy)
+
+    for other, oz, ow in others:
+        spot = {"pts": oz, "view": ow}
+        start(remote(meta.at[me], meta.at[me], meta_s.at[other], meta_r.at[me], spot))
+    for other, oz, ow in others:
+        spot = {"pts": oz, "view": ow}
+        start(remote(kv_out.at[other], kv.at[me], kv_s.at[other], kv_r.at[me], spot))
+    kv[me] = kv_out[me]
+
+    for peer in range(pts):
+        parts = []
+        for half in range(view):
+            at = (peer * view + half) * DH
+            tile = (at // WIDE) * WIDE
+            off = at - tile
+            parts.append((q_ref[:, tile + off : tile + off + DH], g_ref[:, tile + off : tile + off + DH]))
+        qh, gh = parts[0]
+        packed = jnp.concatenate([qh, gh], axis=1)
+        for half in range(1, view):
+            qn, gn = parts[half]
+            packed = jnp.where(w == half, jnp.concatenate([qn, gn], axis=1), packed)
+        qd_out[peer] = packed
+    for oz in column:
+        spot = {"pts": oz, "view": w}
+        start(remote(qd_out.at[oz], qd.at[z], qd_s.at[oz], qd_r.at[z], spot))
+    qd[z] = qd_out[z]
+
+    for other, oz, ow in others:
+        remote(meta.at[me], meta.at[other], meta_s.at[other], meta_r.at[other], {"pts": oz, "view": ow}).wait_recv()
+
+    tile_of = lax.broadcasted_iota(jnp.int32, (META_ROWS, keys), 1) // (keys // (peers * (held // TILE)))
+    for p in range(pts):
+        hit = None
+        for half in range(view):
+            ids = meta[p * view + half]
+            for i in range(nvis):
+                one = ids[:, i : i + 1] == tile_of
+                hit = one if hit is None else hit | one
+        bias[p] = jnp.where(hit, 0.0, HIDDEN)
+    row_number = lax.broadcasted_iota(jnp.int32, (pts * p_dev, WIDE), 0)
+    for p in range(pts):
+        for c in range(dest_rows):
+            line = meta[p * view, qb_dev + c : qb_dev + c + 1, :]
+            at = p * p_dev + c * WIDE
+            place[:, at : at + WIDE] = jnp.where(row_number == line, 1.0, 0.0).astype(jnp.bfloat16)
+
+    for other, oz, ow in others:
+        remote(kv_out.at[0], kv.at[other], kv_s.at[other], kv_r.at[other], {"pts": oz, "view": ow}).wait_recv()
+    grads[...] = jnp.zeros_like(grads)
+
+    lower = lax.broadcasted_iota(jnp.int32, (qblock, WIDE), 1) < DH
+    zero = jnp.zeros((), jnp.bfloat16)
+    scale = DH**-0.5
+    nt = (((1,), (1,)), ((), ()))
+
+    def block(p, b):
+        both = kv[...].reshape(keys, WIDE)
+        mixed = qd[p, b * qblock : (b + 1) * qblock, :]
+        query = jnp.where(lower, mixed * jnp.asarray(scale, jnp.bfloat16), zero)
+        grad = jnp.where(lower, zero, mixed)
+        scores = lax.dot_general(query, both, nt, preferred_element_type=jnp.float32)
+        scores = scores + bias[p, b : b + 1, :]
+        d_prob = lax.dot_general(grad, both, nt, preferred_element_type=jnp.float32)
+        peak = jnp.max(scores, axis=1, keepdims=True)
+        weight = jnp.exp(scores - peak)
+        total = jnp.sum(weight, axis=1, keepdims=True)
+        inverse = 1.0 / total
+        summed = jnp.dot(weight.astype(jnp.bfloat16), both, preferred_element_type=jnp.float32)
+        out = (summed / total).astype(jnp.bfloat16)
+        delta = jnp.sum(
+            grad.astype(jnp.float32) * out.astype(jnp.float32), axis=1, keepdims=True
+        )
+        prob = weight * inverse
+        d_score = (prob * (d_prob - delta)).astype(jnp.bfloat16)
+        d_query = jnp.dot(d_score, both, preferred_element_type=jnp.float32) * scale
+        left = jnp.concatenate([query, grad], axis=0)
+        right = jnp.concatenate([d_score, prob.astype(jnp.bfloat16)], axis=0)
+        grads[...] += jnp.dot(left.T, right, preferred_element_type=jnp.float32)
+        return jnp.where(lower, d_query.astype(jnp.bfloat16), out)
+
+    def step_body(step, carry):
+        p = lax.rem(z + step, pts)
+
+        @pl.when(step > 0)
+        def _():
+            remote(qd_out.at[0], qd.at[p], qd_s.at[p], qd_r.at[p], {"pts": p, "view": w}).wait_recv()
+
+        for b in range(qb_dev):
+            rows[p, b * qblock : (b + 1) * qblock, :] = block(p, b)
+        return carry
+
+    lax.fori_loop(0, pts, step_body, 0)
+
+    dkv_out[...] = grads[...].T.astype(jnp.bfloat16).reshape(dkv_out.shape)
+    for other, oz, ow in others:
+        spot = {"pts": oz, "view": ow}
+        start(remote(dkv_out.at[other], dkv.at[me], dkv_s.at[other], dkv_r.at[me], spot))
+    dkv[me] = dkv_out[me]
+
+    every = rows[...].reshape(pts * p_dev, WIDE)
+    moved = jnp.dot(place[...], every, preferred_element_type=jnp.float32).astype(jnp.bfloat16)
+    lower_all = lax.broadcasted_iota(jnp.int32, (pts * p_dev, WIDE), 1) < DH
+    od_out[...] = jnp.where(lower_all, every, moved).reshape(od_out.shape)
+    for other, oz, ow in others:
+        spot = {"pts": oz, "view": ow}
+        start(remote(od_out.at[oz], od.at[me], od_s.at[other], od_r.at[me], spot))
+    od[me] = od_out[z]
+
+    for other, oz, ow in others:
+        remote(dkv_out.at[0], dkv.at[other], dkv_s.at[other], dkv_r.at[other], {"pts": oz, "view": ow}).wait_recv()
+    for pair in range(peers // 2):
+        cols = slice(pair * WIDE, (pair + 1) * WIDE)
+        even, odd = dkv[2 * pair], dkv[2 * pair + 1]
+        dk_ref[:, cols] = jnp.concatenate([even[:, :DH], odd[:, :DH]], axis=1)
+        dv_ref[:, cols] = jnp.concatenate([even[:, DH:], odd[:, DH:]], axis=1)
+    for other, oz, ow in others:
+        remote(od_out.at[0], od.at[other], od_s.at[other], od_r.at[other], {"pts": oz, "view": ow}).wait_recv()
+    for pair in range(peers // 2):
+        cols = slice(pair * WIDE, (pair + 1) * WIDE)
+        even, odd = od[2 * pair], od[2 * pair + 1]
+        dq_ref[:, cols] = jnp.concatenate([even[:, :DH], odd[:, :DH]], axis=1)
+        att_ref[:, cols] = jnp.concatenate([even[:, DH:], odd[:, DH:]], axis=1)
+    for copy in sends:
+        copy.wait_send()
+
+
+def by_head(queries, key_tiles, value_tiles, visible, destination, d_out):
+    pts = lax.axis_size("pts")
+    view = lax.axis_size("view")
+    peers = pts * view
+    kv_dev, tile_keys, width = key_tiles.shape
+    held = kv_dev * tile_keys
+    p_dev = queries.shape[0]
+    keys = peers * held
+    whole = pl.BlockSpec(memory_space=pltpu.VMEM)
+    bf = jnp.bfloat16
+    dma = pltpu.SemaphoreType.DMA
+    att, dq, dk, dv = pl.pallas_call(
+        functools.partial(head_kernel, pts, view),
+        out_shape=(
+            jax.ShapeDtypeStruct((p_dev, width), bf),
+            jax.ShapeDtypeStruct((p_dev, width), bf),
+            jax.ShapeDtypeStruct((held, width), bf),
+            jax.ShapeDtypeStruct((held, width), bf),
+        ),
+        in_specs=[whole] * 6,
+        out_specs=(whole,) * 4,
+        scratch_shapes=[
+            pltpu.VMEM((peers, META_ROWS, WIDE), jnp.int32),
+            pltpu.VMEM((peers, held, WIDE), bf),
+            pltpu.VMEM((peers, held, WIDE), bf),
+            pltpu.VMEM((pts, p_dev, WIDE), bf),
+            pltpu.VMEM((pts, p_dev, WIDE), bf),
+            pltpu.VMEM((pts, META_ROWS, keys), jnp.float32),
+            pltpu.VMEM((pts * p_dev, pts * p_dev), bf),
+            pltpu.VMEM((pts, p_dev, WIDE), bf),
+            pltpu.VMEM((WIDE, keys), jnp.float32),
+            pltpu.VMEM((pts, p_dev, WIDE), bf),
+            pltpu.VMEM((peers, p_dev, WIDE), bf),
+            pltpu.VMEM((peers, held, WIDE), bf),
+            pltpu.VMEM((peers, held, WIDE), bf),
+            dma((peers,)),
+            dma((peers,)),
+            dma((peers,)),
+            dma((peers,)),
+            dma((pts,)),
+            dma((pts,)),
+            dma((peers,)),
+            dma((peers,)),
+            dma((peers,)),
+            dma((peers,)),
+        ],
+        compiler_params=pltpu.CompilerParams(
+            collective_id=0, has_side_effects=True, vmem_limit_bytes=48 * 1024 * 1024
+        ),
+        cost_estimate=pl.CostEstimate(
+            flops=14 * pts * p_dev * keys * DH,
+            bytes_accessed=6 * p_dev * width * 2,
+            transcendentals=pts * p_dev * keys,
+        ),
+    )(
+        queries,
+        key_tiles.reshape(held, width),
+        value_tiles.reshape(held, width),
+        visible,
+        destination.reshape(p_dev // WIDE, WIDE),
+        d_out,
+    )
+    return (att, dq, dk.reshape(key_tiles.shape), dv.reshape(value_tiles.shape))
+
+
 def solution(mesh):
     in_specs = (
         P(("scene", "pts"), "head"),
@@ -258,4 +558,8 @@
         P(("scene", "pts", "view"), None, "head"),
         P(("scene", "pts", "view"), None, "head"),
     )
-    return jax.shard_map(local, mesh=mesh, in_specs=in_specs, out_specs=out_specs, check_vma=False)
+    heads_local = HEADS // mesh.shape["head"]
+    per_device = local
+    if heads_local == mesh.shape["pts"] * mesh.shape["view"] and heads_local % 2 == 0:
+        per_device = by_head
+    return jax.shard_map(per_device, mesh=mesh, in_specs=in_specs, out_specs=out_specs, check_vma=False)

time: 161 us -> 47.6 us (0.30)
  the two profiles are of different devices: /device:TPU:0 before, /device:TPU:31 now
where the time goes in v1:
time: 47.6 us; the launch traced here: 47.4 us
  Pallas kernels  39.6 us (83%)
  local copies, waits for them, and re-layouts  7.1 us (15%)
  between operations  0.66 us (1%)
    pallas_call x1, Pallas kernels, by_head(): pl.pallas_call(functools.partial(head_kernel, pts, view), out_shape=(jax....  39.6 us
    unnamed x16, local copies, waits for them, and re-layouts  7.1 us

profile of v1, /device:TPU:31, one launch (start us, length us, event | category | flops | bytes accessed | tf_op | source)
XLA Modules:
  0.0 47.4 jit_solution(16025947469139672000)
XLA Ops:
  0.6 0.0 copy-start.5
  0.6 0.0 copy-start.4
  0.7 0.7 %copy-done.5 = s32[256]{0:T(256)S(1)} copy-done((s32[256]{0:T(256)S(1)}, s32[256]{0:T(256)}, u32[]{:S(2)}) %copy-start.5) | copy-done | bytes 1048
  1.3 0.0 copy-done.4
  1.3 0.0 copy-start
  1.3 0.9 %copy-done = bf16[256,512]{1,0:T(8,128)(2,1)S(1)} copy-done((bf16[256,512]{1,0:T(8,128)(2,1)S(1)}, bf16[256,512]{1,0:T(8,128)(2,1)}, u32[]{:S(2)}) %copy-start) | copy-done | bytes 262168
  2.3 0.0 copy-start.1
  2.3 0.9 %copy-done.1 = bf16[256,512]{1,0:T(8,128)(2,1)S(1)} copy-done((bf16[256,512]{1,0:T(8,128)(2,1)S(1)}, bf16[256,512]{1,0:T(8,128)(2,1)}, u32[]{:S(2)}) %copy-start.1) | copy-done | bytes 262168
  3.2 0.0 copy-start.2
  3.2 0.9 %copy-done.2 = bf16[8,16,512]{2,1,0:T(8,128)(2,1)S(1)} copy-done((bf16[8,16,512]{2,1,0:T(8,128)(2,1)S(1)}, bf16[8,16,512]{2,1,0:T(8,128)(2,1)}, u32[]{:S(2)}) %copy-start.2) | copy-done | bytes 131096
  4.1 0.0 copy-start.3
  4.1 0.9 %copy-done.3 = bf16[8,16,512]{2,1,0:T(8,128)(2,1)S(1)} copy-done((bf16[8,16,512]{2,1,0:T(8,128)(2,1)S(1)}, bf16[8,16,512]{2,1,0:T(8,128)(2,1)}, u32[]{:S(2)}) %copy-start.3) | copy-done | bytes 131096
  5.0 39.6 %shard_map.93 = (bf16[256,512]{1,0:T(8,128)(2,1)S(1)}, bf16[256,512]{1,0:T(8,128)(2,1)S(1)}, bf16[128,512]{1,0:T(8,128)(2,1)S(1)}, bf16[128,512]{1,0:T(8,128)(2,1)S(1)}) custom-call(bf16[256,512]{1,0:T(8,128)(2,1)S(1)} %copy-done, bf16[128,512]{1,0:T(8,128)(2,1)S(1)} %bitcast.7, bf16[128,512]{1,0:T(8,128)(2,1)S(1)} %bitcast.8, s32[2,16]{1,0:T(2,128)S(1)} %copy-done.4, ...), custom_call_target="tpu_custom_call" | custom-call | flops 939524096 | bytes 1572864 | tf_op jit(solution)/shard_map/pallas_call | solution.py:492
  44.6 0.7 %copy.14 = bf16[256,512]{1,0:T(8,128)(2,1)} copy(bf16[256,512]{1,0:T(8,128)(2,1)S(1)} %get-tuple-element.16) | data formatting | bytes 524288
  45.3 0.7 %copy.15 = bf16[256,512]{1,0:T(8,128)(2,1)} copy(bf16[256,512]{1,0:T(8,128)(2,1)S(1)} %get-tuple-element.17) | data formatting | bytes 524288
  46.0 0.7 %copy.16 = bf16[8,16,512]{2,1,0:T(8,128)(2,1)} copy(bf16[8,16,512]{2,1,0:T(8,128)(2,1)S(1)} %bitcast.6) | data formatting | bytes 262144
  46.7 0.7 %copy.17 = bf16[8,16,512]{2,1,0:T(8,128)(2,1)} copy(bf16[8,16,512]{2,1,0:T(8,128)(2,1)S(1)} %bitcast.5) | data formatting | bytes 262144
Async XLA Ops:
  0.6 0.7 %copy-start.5 = (s32[256]{0:T(256)S(1)}, s32[256]{0:T(256)}, u32[]{:S(2)}) copy-start(s32[256]{0:T(256)} %param.10) | copy-start | bytes 3076
  0.6 0.7 %copy-start.4 = (s32[2,16]{1,0:T(2,128)S(1)}, s32[2,16]{1,0:T(2,128)}, u32[]{:S(2)}) copy-start(s32[2,16]{1,0:T(2,128)} %vis_ref.1) | copy-start | bytes 388
  1.3 0.9 %copy-start = (bf16[256,512]{1,0:T(8,128)(2,1)S(1)}, bf16[256,512]{1,0:T(8,128)(2,1)}, u32[]{:S(2)}) copy-start(bf16[256,512]{1,0:T(8,128)(2,1)} %q_ref.1) | copy-start | bytes 786436
  2.3 0.9 %copy-start.1 = (bf16[256,512]{1,0:T(8,128)(2,1)S(1)}, bf16[256,512]{1,0:T(8,128)(2,1)}, u32[]{:S(2)}) copy-start(bf16[256,512]{1,0:T(8,128)(2,1)} %g_ref.1) | copy-start | bytes 786436
  3.2 0.9 %copy-start.2 = (bf16[8,16,512]{2,1,0:T(8,128)(2,1)S(1)}, bf16[8,16,512]{2,1,0:T(8,128)(2,1)}, u32[]{:S(2)}) copy-start(bf16[8,16,512]{2,1,0:T(8,128)(2,1)} %param.7) | copy-start | bytes 393220
  4.1 0.9 %copy-start.3 = (bf16[8,16,512]{2,1,0:T(8,128)(2,1)S(1)}, bf16[8,16,512]{2,1,0:T(8,128)(2,1)}, u32[]{:S(2)}) copy-start(bf16[8,16,512]{2,1,0:T(8,128)(2,1)} %param.8) | copy-start | bytes 393220

commit v2 on v1

--- a/solution.py
+++ b/solution.py
@@ -264,6 +264,7 @@
 WIDE = 2 * DH
 TILE = 16
 HIDDEN = -1e30
+ROOM = 63 * 1024 * 1024
 META_ROWS = 8
 
 
@@ -281,16 +282,21 @@
 def head_kernel(
     pts,
     view,
+    q_hbm,
+    k_hbm,
+    v_hbm,
+    vis_hbm,
+    dest_hbm,
+    g_hbm,
+    att,
+    dq,
+    dkv,
     q_ref,
     k_ref,
     v_ref,
     vis_ref,
     dest_ref,
     g_ref,
-    att_ref,
-    dq_ref,
-    dk_ref,
-    dv_ref,
     meta,
     kv_out,
     kv,
@@ -300,18 +306,20 @@
     place,
     rows,
     grads,
-    od_out,
-    od,
+    att_out,
+    dq_out,
     dkv_out,
-    dkv,
+    load_s,
     meta_s,
     meta_r,
     kv_s,
     kv_r,
     qd_s,
     qd_r,
-    od_s,
-    od_r,
+    att_s,
+    att_r,
+    dq_s,
+    dq_r,
     dkv_s,
     dkv_r,
 ):
@@ -337,7 +345,22 @@
     for _, oz, ow in others:
         pl.semaphore_signal(barrier, inc=1, device_id={"pts": oz, "view": ow}, device_id_type=MESH)
 
+    loads = []
+    pairs = (
+        (k_hbm, k_ref),
+        (v_hbm, v_ref),
+        (vis_hbm, vis_ref),
+        (dest_hbm, dest_ref),
+        (q_hbm, q_ref),
+        (g_hbm, g_ref),
+    )
+    for number, (source, target) in enumerate(pairs):
+        load = pltpu.make_async_copy(source, target, load_s.at[number])
+        load.start()
+        loads.append(load)
     meta[me] = jnp.zeros((META_ROWS, WIDE), jnp.int32)
+    for load in loads[:4]:
+        load.wait()
     meta[me, 0:qb_dev, 0:nvis] = vis_ref[...]
     meta[me, qb_dev : qb_dev + dest_rows, :] = dest_ref[...]
     for pair in range(peers // 2):
@@ -360,6 +383,8 @@
         spot = {"pts": oz, "view": ow}
         start(remote(kv_out.at[other], kv.at[me], kv_s.at[other], kv_r.at[me], spot))
     kv[me] = kv_out[me]
+    for load in loads[4:]:
+        load.wait()
 
     for peer in range(pts):
         parts = []
@@ -432,6 +457,20 @@
         grads[...] += jnp.dot(left.T, right, preferred_element_type=jnp.float32)
         return jnp.where(lower, d_query.astype(jnp.bfloat16), out)
 
+    half_rows = p_dev // 2
+    twin = {"pts": z, "view": lax.rem(w + 1, view)}
+
+    def fold(upper, lower_half, side):
+        at = slice(side * DH, (side + 1) * DH)
+        return jnp.concatenate([upper[:, at], lower_half[:, at]], axis=1)
+
+    def dq_copy(p):
+        spot = {"pts": p, "view": w}
+        return remote(dq_out.at[p], dq.at[me], dq_s.at[p], dq_r.at[me], spot)
+
+    def twin_copy(source, target, sent, got, number):
+        return remote(source, target.at[number], sent, got.at[number], twin)
+
     def step_body(step, carry):
         p = lax.rem(z + step, pts)
 
@@ -441,41 +480,101 @@
 
         for b in range(qb_dev):
             rows[p, b * qblock : (b + 1) * qblock, :] = block(p, b)
+        dq_out[p] = fold(rows[p, :half_rows, :], rows[p, half_rows:, :], 0)
+
+        @pl.when(step > 0)
+        def _():
+            dq_copy(p).start()
+
         return carry
 
     lax.fori_loop(0, pts, step_body, 0)
-
-    dkv_out[...] = grads[...].T.astype(jnp.bfloat16).reshape(dkv_out.shape)
-    for other, oz, ow in others:
-        spot = {"pts": oz, "view": ow}
-        start(remote(dkv_out.at[other], dkv.at[me], dkv_s.at[other], dkv_r.at[me], spot))
-    dkv[me] = dkv_out[me]
-
-    every = rows[...].reshape(pts * p_dev, WIDE)
-    moved = jnp.dot(place[...], every, preferred_element_type=jnp.float32).astype(jnp.bfloat16)
-    lower_all = lax.broadcasted_iota(jnp.int32, (pts * p_dev, WIDE), 1) < DH
-    od_out[...] = jnp.where(lower_all, every, moved).reshape(od_out.shape)
-    for other, oz, ow in others:
-        spot = {"pts": oz, "view": ow}
-        start(remote(od_out.at[oz], od.at[me], od_s.at[other], od_r.at[me], spot))
-    od[me] = od_out[z]
-
-    for other, oz, ow in others:
-        remote(dkv_out.at[0], dkv.at[other], dkv_s.at[other], dkv_r.at[other], {"pts": oz, "view": ow}).wait_recv()
-    for pair in range(peers // 2):
-        cols = slice(pair * WIDE, (pair + 1) * WIDE)
-        even, odd = dkv[2 * pair], dkv[2 * pair + 1]
-        dk_ref[:, cols] = jnp.concatenate([even[:, :DH], odd[:, :DH]], axis=1)
-        dv_ref[:, cols] = jnp.concatenate([even[:, DH:], odd[:, DH:]], axis=1)
-    for other, oz, ow in others:
-        remote(od_out.at[0], od.at[other], od_s.at[other], od_r.at[other], {"pts": oz, "view": ow}).wait_recv()
-    for pair in range(peers // 2):
-        cols = slice(pair * WIDE, (pair + 1) * WIDE)
-        even, odd = od[2 * pair], od[2 * pair + 1]
-        dq_ref[:, cols] = jnp.concatenate([even[:, :DH], odd[:, :DH]], axis=1)
-        att_ref[:, cols] = jnp.concatenate([even[:, DH:], odd[:, DH:]], axis=1)
+    kept = []
+    start(twin_copy(dq_out.at[z], dq, dq_s.at[z], dq_r, me))
+    dq_own = pltpu.make_async_copy(dq_out.at[z], dq.at[me], load_s.at[0])
+    dq_own.start()
+    kept.append(dq_own)
+
+    def send_att():
+        every = rows[...].reshape(pts * p_dev, WIDE)
+        moved = jnp.dot(place[...], every, preferred_element_type=jnp.float32)
+        for p in range(pts):
+            top = moved[p * p_dev : p * p_dev + half_rows]
+            low = moved[p * p_dev + half_rows : (p + 1) * p_dev]
+            att_out[p] = fold(top, low, 1).astype(jnp.bfloat16)
+        for oz in column:
+            spot = {"pts": oz, "view": w}
+            start(remote(att_out.at[oz], att.at[me], att_s.at[oz], att_r.at[me], spot))
+        start(twin_copy(att_out.at[z], att, att_s.at[z], att_r, me))
+        att_own = pltpu.make_async_copy(att_out.at[z], att.at[me], load_s.at[1])
+        att_own.start()
+        kept.append(att_own)
+
+    def send_dkv():
+        dkv_out[...] = grads[...].T.astype(jnp.bfloat16).reshape(dkv_out.shape)
+        for other, oz, ow in others:
+            spot = {"pts": oz, "view": ow}
+            start(remote(dkv_out.at[other], dkv.at[me], dkv_s.at[other], dkv_r.at[me], spot))
+        dkv_own = pltpu.make_async_copy(dkv_out.at[me], dkv.at[me], load_s.at[2])
+        dkv_own.start()
+        kept.append(dkv_own)
+
+    send_att()
+    send_dkv()
+
+    def arrived(buffer, sent, got, number):
+        source = att_out.at[0] if buffer is not dkv else dkv_out.at[0]
+        remote(source, buffer.at[number], sent.at[0], got.at[number], twin).wait_recv()
+
+    for oz in column:
+        number = oz * view + w
+        arrived(dq, dq_s, dq_r, number)
+        start(twin_copy(dq.at[number], dq, dq_s.at[pts + oz], dq_r, number))
+    for oz in column:
+        number = oz * view + w
+        arrived(att, att_s, att_r, number)
+        start(twin_copy(att.at[number], att, att_s.at[pts + oz], att_r, number))
+    for other, _, _ in others:
+        arrived(dkv, dkv_s, dkv_r, other)
+    for oz in range(pts):
+        number = oz * view + lax.rem(w + 1, view)
+        arrived(dq, dq_s, dq_r, number)
+        arrived(att, att_s, att_r, number)
+    for oz in column:
+        dq_copy(oz).wait_send()
     for copy in sends:
         copy.wait_send()
+    for copy in kept:
+        copy.wait()
+
+
+def unpack_kernel(att, dq, dkv, att_hbm, dq_hbm, dk_hbm, dv_hbm, att_ref, dq_ref, dk_ref, dv_ref, sems):
+    peers = att.shape[0]
+    half_rows = att.shape[1]
+
+    def write(source, target, number):
+        copy = pltpu.make_async_copy(source, target, sems.at[number])
+        copy.start()
+        return copy
+
+    def two(buffer, pair, side):
+        at = slice(side * DH, (side + 1) * DH)
+        return jnp.concatenate([buffer[2 * pair][:, at], buffer[2 * pair + 1][:, at]], axis=1)
+
+    copies = []
+    for number, (buffer, ref, out) in enumerate(((att, att_ref, att_hbm), (dq, dq_ref, dq_hbm))):
+        for pair in range(peers // 2):
+            cols = slice(pair * WIDE, (pair + 1) * WIDE)
+            ref[:half_rows, cols] = two(buffer, pair, 0)
+            ref[half_rows:, cols] = two(buffer, pair, 1)
+        copies.append(write(ref, out, number))
+    for side, (ref, out) in enumerate(((dk_ref, dk_hbm), (dv_ref, dv_hbm))):
+        for pair in range(peers // 2):
+            cols = slice(pair * WIDE, (pair + 1) * WIDE)
+            ref[:, cols] = two(dkv, pair, side)
+        copies.append(write(ref, out, 2 + side))
+    for copy in copies:
+        copy.wait()
 
 
 def by_head(queries, key_tiles, value_tiles, visible, destination, d_out):
@@ -489,58 +588,77 @@
     whole = pl.BlockSpec(memory_space=pltpu.VMEM)
     bf = jnp.bfloat16
     dma = pltpu.SemaphoreType.DMA
-    att, dq, dk, dv = pl.pallas_call(
+    anywhere = pl.BlockSpec(memory_space=pltpu.HBM)
+    vmem = pltpu.VMEM
+    operands = (
+        queries,
+        key_tiles.reshape(held, width),
+        value_tiles.reshape(held, width),
+        visible,
+        destination.reshape(p_dev // WIDE, WIDE),
+        d_out,
+    )
+    landed = (
+        jax.ShapeDtypeStruct((peers, p_dev // 2, WIDE), bf),
+        jax.ShapeDtypeStruct((peers, p_dev // 2, WIDE), bf),
+        jax.ShapeDtypeStruct((peers, held, WIDE), bf),
+    )
+    att, dq, dkv = pl.pallas_call(
         functools.partial(head_kernel, pts, view),
-        out_shape=(
-            jax.ShapeDtypeStruct((p_dev, width), bf),
-            jax.ShapeDtypeStruct((p_dev, width), bf),
-            jax.ShapeDtypeStruct((held, width), bf),
-            jax.ShapeDtypeStruct((held, width), bf),
-        ),
-        in_specs=[whole] * 6,
-        out_specs=(whole,) * 4,
-        scratch_shapes=[
-            pltpu.VMEM((peers, META_ROWS, WIDE), jnp.int32),
-            pltpu.VMEM((peers, held, WIDE), bf),
-            pltpu.VMEM((peers, held, WIDE), bf),
-            pltpu.VMEM((pts, p_dev, WIDE), bf),
-            pltpu.VMEM((pts, p_dev, WIDE), bf),
-            pltpu.VMEM((pts, META_ROWS, keys), jnp.float32),
-            pltpu.VMEM((pts * p_dev, pts * p_dev), bf),
-            pltpu.VMEM((pts, p_dev, WIDE), bf),
-            pltpu.VMEM((WIDE, keys), jnp.float32),
-            pltpu.VMEM((pts, p_dev, WIDE), bf),
-            pltpu.VMEM((peers, p_dev, WIDE), bf),
-            pltpu.VMEM((peers, held, WIDE), bf),
-            pltpu.VMEM((peers, held, WIDE), bf),
+        out_shape=landed,
+        in_specs=[anywhere] * 6,
+        out_specs=(anywhere,) * 3,
+        scratch_shapes=[vmem(x.shape, x.dtype) for x in operands]
+        + [
+            vmem((peers, META_ROWS, WIDE), jnp.int32),
+            vmem((peers, held, WIDE), bf),
+            vmem((peers, held, WIDE), bf),
+            vmem((pts, p_dev, WIDE), bf),
+            vmem((pts, p_dev, WIDE), bf),
+            vmem((pts, META_ROWS, keys), jnp.float32),
+            vmem((pts * p_dev, pts * p_dev), bf),
+            vmem((pts, p_dev, WIDE), bf),
+            vmem((WIDE, keys), jnp.float32),
+            vmem((pts, p_dev // 2, WIDE), bf),
+            vmem((pts, p_dev // 2, WIDE), bf),
+            vmem((peers, held, WIDE), bf),
+            dma((6,)),
             dma((peers,)),
             dma((peers,)),
             dma((peers,)),
             dma((peers,)),
             dma((pts,)),
             dma((pts,)),
-            dma((peers,)),
+            dma((2 * pts,)),
+            dma((peers,)),
+            dma((2 * pts,)),
             dma((peers,)),
             dma((peers,)),
             dma((peers,)),
         ],
         compiler_params=pltpu.CompilerParams(
-            collective_id=0, has_side_effects=True, vmem_limit_bytes=48 * 1024 * 1024
+            collective_id=0, has_side_effects=True, vmem_limit_bytes=ROOM
         ),
         cost_estimate=pl.CostEstimate(
             flops=14 * pts * p_dev * keys * DH,
             bytes_accessed=6 * p_dev * width * 2,
             transcendentals=pts * p_dev * keys,
         ),
-    )(
-        queries,
-        key_tiles.reshape(held, width),
-        value_tiles.reshape(held, width),
-        visible,
-        destination.reshape(p_dev // WIDE, WIDE),
-        d_out,
-    )
-    return (att, dq, dk.reshape(key_tiles.shape), dv.reshape(value_tiles.shape))
+    )(*operands)
+    finals = [(p_dev, width), (p_dev, width), (held, width), (held, width)]
+    attended, d_queries, d_keys, d_values = pl.pallas_call(
+        unpack_kernel,
+        out_shape=tuple(jax.ShapeDtypeStruct(shape, bf) for shape in finals),
+        in_specs=[whole] * 3,
+        out_specs=(anywhere,) * 4,
+        scratch_shapes=[vmem(shape, bf) for shape in finals] + [dma((4,))],
+    )(att, dq, dkv)
+    return (
+        attended,
+        d_queries,
+        d_keys.reshape(key_tiles.shape),
+        d_values.reshape(value_tiles.shape),
+    )
 
 
 def solution(mesh):
@@ -560,6 +678,6 @@
     )
     heads_local = HEADS // mesh.shape["head"]
     per_device = local
-    if heads_local == mesh.shape["pts"] * mesh.shape["view"] and heads_local % 2 == 0:
+    if heads_local == mesh.shape["pts"] * mesh.shape["view"] and mesh.shape["view"] == 2:
         per_device = by_head
     return jax.shard_map(per_device, mesh=mesh, in_specs=in_specs, out_specs=out_specs, check_vma=False)

time: 47.6 us -> 37.7 us (0.79)
  the two profiles are of different devices: /device:TPU:31 before, /device:TPU:0 now
where the time goes in v2:
time: 37.7 us; the launch traced here: 37.5 us
  Pallas kernels  36.9 us (98%)
  between operations  0.64 us (2%)
    pallas_call x1, Pallas kernels, by_head(): pl.pallas_call(functools.partial(head_kernel, pts, view), out_shape=lande...  34.7 us
    pallas_call x1, Pallas kernels, by_head(): pl.pallas_call(unpack_kernel, out_shape=tuple((jax.ShapeDtypeStruct(shape...  2.15 us

profile of v2, /device:TPU:0, one launch (start us, length us, event | category | flops | bytes accessed | tf_op | source)
XLA Modules:
  0.0 37.5 jit_solution(18070772772849409853)
XLA Ops:
  0.6 34.7 %shard_map.93 = (bf16[8,128,128]{2,1,0:T(8,128)(2,1)}, bf16[8,128,128]{2,1,0:T(8,128)(2,1)}, bf16[8,128,128]{2,1,0:T(8,128)(2,1)}) custom-call(bf16[256,512]{1,0:T(8,128)(2,1)} %q_hbm.1, bf16[128,512]{1,0:T(8,128)(2,1)} %bitcast.5, bf16[128,512]{1,0:T(8,128)(2,1)} %bitcast.6, s32[2,16]{1,0:T(2,128)} %vis_hbm.1, s32[2,128]{1,0:T(2,128)} %bitcast.9, ...), custom_call_target="tpu_custom_call" | custom-call | flops 939524096 | bytes 1572864 | tf_op jit(solution)/shard_map/pallas_call | solution.py:606
  35.4 2.1 %shard_map.94 = (bf16[256,512]{1,0:T(8,128)(2,1)}, bf16[256,512]{1,0:T(8,128)(2,1)}, bf16[128,512]{1,0:T(8,128)(2,1)}, bf16[128,512]{1,0:T(8,128)(2,1)}) custom-call(bf16[8,128,128]{2,1,0:T(8,128)(2,1)} %get-tuple-element.11.att, bf16[8,128,128]{2,1,0:T(8,128)(2,1)} %get-tuple-element.12.dq, bf16[8,128,128]{2,1,0:T(8,128)(2,1)} %get-tuple-element.13.dkv), custom_call_target="tpu_custom_call" | custom-call | tf_op jit(solution)/shard_map/pallas_call | solution.py:649

commit v3 on v2

--- a/solution.py
+++ b/solution.py
@@ -266,6 +266,14 @@
 HIDDEN = -1e30
 ROOM = 63 * 1024 * 1024
 META_ROWS = 8
+
+
+def partner(z, step, pts):
+    found, unit = 0, 1
+    while unit < pts:
+        found = found + unit * lax.rem(z // unit + step // unit, 2)
+        unit *= 2
+    return found
 
 
 def remote(src, dst, send_sem, recv_sem, place):
@@ -341,7 +349,7 @@
         others.append((other, other // view, lax.rem(other, view)))
     column = []
     for step in range(1, pts):
-        column.append(lax.rem(z + step, pts))
+        column.append(partner(z, step, pts))
     for _, oz, ow in others:
         pl.semaphore_signal(barrier, inc=1, device_id={"pts": oz, "view": ow}, device_id_type=MESH)
 
@@ -427,18 +435,22 @@
         remote(kv_out.at[0], kv.at[other], kv_s.at[other], kv_r.at[other], {"pts": oz, "view": ow}).wait_recv()
     grads[...] = jnp.zeros_like(grads)
 
-    lower = lax.broadcasted_iota(jnp.int32, (qblock, WIDE), 1) < DH
+    lower = lax.broadcasted_iota(jnp.int32, (p_dev, WIDE), 1) < DH
     zero = jnp.zeros((), jnp.bfloat16)
     scale = DH**-0.5
     nt = (((1,), (1,)), ((), ()))
 
-    def block(p, b):
+    def shade(p):
+        lines = [jnp.broadcast_to(bias[p, b : b + 1, :], (qblock, keys)) for b in range(qb_dev)]
+        return jnp.concatenate(lines, axis=0)
+
+    def block(p):
         both = kv[...].reshape(keys, WIDE)
-        mixed = qd[p, b * qblock : (b + 1) * qblock, :]
+        mixed = qd[p]
         query = jnp.where(lower, mixed * jnp.asarray(scale, jnp.bfloat16), zero)
         grad = jnp.where(lower, zero, mixed)
         scores = lax.dot_general(query, both, nt, preferred_element_type=jnp.float32)
-        scores = scores + bias[p, b : b + 1, :]
+        scores = scores + shade(p)
         d_prob = lax.dot_general(grad, both, nt, preferred_element_type=jnp.float32)
         peak = jnp.max(scores, axis=1, keepdims=True)
         weight = jnp.exp(scores - peak)
@@ -472,23 +484,21 @@
         return remote(source, target.at[number], sent, got.at[number], twin)
 
     def step_body(step, carry):
-        p = lax.rem(z + step, pts)
-
-        @pl.when(step > 0)
-        def _():
+        p = partner(z, step, pts)
+
+        if step > 0:
             remote(qd_out.at[0], qd.at[p], qd_s.at[p], qd_r.at[p], {"pts": p, "view": w}).wait_recv()
 
-        for b in range(qb_dev):
-            rows[p, b * qblock : (b + 1) * qblock, :] = block(p, b)
+        rows[p] = block(p)
         dq_out[p] = fold(rows[p, :half_rows, :], rows[p, half_rows:, :], 0)
 
-        @pl.when(step > 0)
-        def _():
+        if step > 0:
             dq_copy(p).start()
 
         return carry
 
-    lax.fori_loop(0, pts, step_body, 0)
+    for step in range(pts):
+        step_body(step, 0)
     kept = []
     start(twin_copy(dq_out.at[z], dq, dq_s.at[z], dq_r, me))
     dq_own = pltpu.make_async_copy(dq_out.at[z], dq.at[me], load_s.at[0])
@@ -678,6 +688,8 @@
     )
     heads_local = HEADS // mesh.shape["head"]
     per_device = local
-    if heads_local == mesh.shape["pts"] * mesh.shape["view"] and mesh.shape["view"] == 2:
+    pts = mesh.shape["pts"]
+    paired = mesh.shape["view"] == 2 and pts & (pts - 1) == 0
+    if paired and heads_local == pts * mesh.shape["view"]:
         per_device = by_head
     return jax.shard_map(per_device, mesh=mesh, in_specs=in_specs, out_specs=out_specs, check_vma=False)

time: 37.7 us -> 35.3 us (0.936)
  Pallas kernels: 36.9 us -> 34.5 us
    pallas_call x1, Pallas kernels: 34.7 us -> 32.4 us  [by_head(): pl.pallas_call(functools.partial(head_kernel, pts, view), out_shape=lande...]
where the time goes in v3:
time: 35.3 us; the launch traced here: 35.2 us
  Pallas kernels  34.5 us (98%)
  between operations  0.64 us (2%)
    pallas_call x1, Pallas kernels, by_head(): pl.pallas_call(functools.partial(head_kernel, pts, view), out_shape=lande...  32.4 us
    pallas_call x1, Pallas kernels, by_head(): pl.pallas_call(unpack_kernel, out_shape=tuple((jax.ShapeDtypeStruct(shape...  2.15 us

profile of v3, /device:TPU:0, one launch (start us, length us, event | category | flops | bytes accessed | tf_op | source)
XLA Modules:
  0.0 35.2 jit_solution(6940816340995186304)
XLA Ops:
  0.6 32.4 %shard_map.93 = (bf16[8,128,128]{2,1,0:T(8,128)(2,1)}, bf16[8,128,128]{2,1,0:T(8,128)(2,1)}, bf16[8,128,128]{2,1,0:T(8,128)(2,1)}) custom-call(bf16[256,512]{1,0:T(8,128)(2,1)} %q_hbm.1, bf16[128,512]{1,0:T(8,128)(2,1)} %bitcast.5, bf16[128,512]{1,0:T(8,128)(2,1)} %bitcast.6, s32[2,16]{1,0:T(2,128)} %vis_hbm.1, s32[2,128]{1,0:T(2,128)} %bitcast.9, ...), custom_call_target="tpu_custom_call" | custom-call | flops 939524096 | bytes 1572864 | tf_op jit(solution)/shard_map/pallas_call | solution.py:616
  33.0 2.1 %shard_map.94 = (bf16[256,512]{1,0:T(8,128)(2,1)}, bf16[256,512]{1,0:T(8,128)(2,1)}, bf16[128,512]{1,0:T(8,128)(2,1)}, bf16[128,512]{1,0:T(8,128)(2,1)}) custom-call(bf16[8,128,128]{2,1,0:T(8,128)(2,1)} %get-tuple-element.11.att, bf16[8,128,128]{2,1,0:T(8,128)(2,1)} %get-tuple-element.12.dq, bf16[8,128,128]{2,1,0:T(8,128)(2,1)} %get-tuple-element.13.dkv), custom_call_target="tpu_custom_call" | custom-call | tf_op jit(solution)/shard_map/pallas_call | solution.py:659

commit v4 on v3

--- a/solution.py
+++ b/solution.py
@@ -345,7 +345,7 @@
     barrier = pltpu.get_barrier_semaphore()
     others = []
     for step in range(1, peers):
-        other = lax.rem(me + step, peers)
+        other = partner(me, peers - step, peers)
         others.append((other, other // view, lax.rem(other, view)))
     column = []
     for step in range(1, pts):
@@ -457,7 +457,7 @@
         total = jnp.sum(weight, axis=1, keepdims=True)
         inverse = 1.0 / total
         summed = jnp.dot(weight.astype(jnp.bfloat16), both, preferred_element_type=jnp.float32)
-        out = (summed / total).astype(jnp.bfloat16)
+        out = (summed * inverse).astype(jnp.bfloat16)
         delta = jnp.sum(
             grad.astype(jnp.float32) * out.astype(jnp.float32), axis=1, keepdims=True
         )
@@ -494,13 +494,14 @@
 
         if step > 0:
             dq_copy(p).start()
+        else:
+            start(twin_copy(dq_out.at[z], dq, dq_s.at[z], dq_r, me))
 
         return carry
 
     for step in range(pts):
         step_body(step, 0)
     kept = []
-    start(twin_copy(dq_out.at[z], dq, dq_s.at[z], dq_r, me))
     dq_own = pltpu.make_async_copy(dq_out.at[z], dq.at[me], load_s.at[0])
     dq_own.start()
     kept.append(dq_own)

time: 35.3 us -> 35.1 us (level)
  no operation moved by 1% of the time
where the time goes in v4:
time: 35.1 us; the launch traced here: 35 us
  Pallas kernels  34.3 us (98%)
  between operations  0.64 us (2%)
    pallas_call x1, Pallas kernels, by_head(): pl.pallas_call(functools.partial(head_kernel, pts, view), out_shape=lande...  32.2 us
    pallas_call x1, Pallas kernels, by_head(): pl.pallas_call(unpack_kernel, out_shape=tuple((jax.ShapeDtypeStruct(shape...  2.15 us

profile of v4, /device:TPU:0, one launch (start us, length us, event | category | flops | bytes accessed | tf_op | source)
XLA Modules:
  0.0 35.0 jit_solution(14708313476621531593)
XLA Ops:
  0.6 32.2 %shard_map.93 = (bf16[8,128,128]{2,1,0:T(8,128)(2,1)}, bf16[8,128,128]{2,1,0:T(8,128)(2,1)}, bf16[8,128,128]{2,1,0:T(8,128)(2,1)}) custom-call(bf16[256,512]{1,0:T(8,128)(2,1)} %q_hbm.1, bf16[128,512]{1,0:T(8,128)(2,1)} %bitcast.5, bf16[128,512]{1,0:T(8,128)(2,1)} %bitcast.6, s32[2,16]{1,0:T(2,128)} %vis_hbm.1, s32[2,128]{1,0:T(2,128)} %bitcast.9, ...), custom_call_target="tpu_custom_call" | custom-call | flops 939524096 | bytes 1572864 | tf_op jit(solution)/shard_map/pallas_call | solution.py:617
  32.8 2.1 %shard_map.94 = (bf16[256,512]{1,0:T(8,128)(2,1)}, bf16[256,512]{1,0:T(8,128)(2,1)}, bf16[128,512]{1,0:T(8,128)(2,1)}, bf16[128,512]{1,0:T(8,128)(2,1)}) custom-call(bf16[8,128,128]{2,1,0:T(8,128)(2,1)} %get-tuple-element.11.att, bf16[8,128,128]{2,1,0:T(8,128)(2,1)} %get-tuple-element.12.dq, bf16[8,128,128]{2,1,0:T(8,128)(2,1)} %get-tuple-element.13.dkv), custom_call_target="tpu_custom_call" | custom-call | tf_op jit(solution)/shard_map/pallas_call | solution.py:660
